TPU v7x, 128 devices: a whole 4x4x4 slice. The times are simulated.
128 devices in a mesh: dp: 4 (over x), ctx: 32 (over z, y, core).
Axes of the slice: x: 4, y: 4, z: 4, core: 2. Of those that a mesh axis runs over, the one named last changes fastest.
Arguments:
- inputs: bfloat16 [16384, 896], P(('dp', 'ctx')), may hold values from -6 to 6
- cotangent: bfloat16 [16384, 896], P(('dp', 'ctx')), may hold values from -6 to 6
- span_order: int32 [64], replicated, may hold values from 0 to 63, as said below
- positions: int32 [16384], P(('dp', 'ctx')), may hold values from 0 to 1023, as said below
- attn_gain: bfloat16 [896], P('dp'), may hold values from 0.5 to 1.5
- qkv_weight: bfloat16 [896, 1152], P('dp'), may hold values from -0.1875 to 0.1875
- qkv_bias: bfloat16 [1152], P('dp'), may hold values from -3 to 3
- out_weight: bfloat16 [896, 896], P('dp'), may hold values from -0.375 to 0.375
- mlp_gain: bfloat16 [896], P('dp'), may hold values from 0.5 to 1.5
- gate_weight: bfloat16 [896, 4864], P('dp'), may hold values from -0.1875 to 0.1875
- up_weight: bfloat16 [896, 4864], P('dp'), may hold values from -0.1875 to 0.1875
- down_weight: bfloat16 [4864, 896], P('dp'), may hold values from -0.078125 to 0.078125
Outputs:
- output: bfloat16 [16384, 896], P(('dp', 'ctx'))
- input_grad: bfloat16 [16384, 896], P(('dp', 'ctx'))
- attn_gain_grad: float32 [896], P('dp')
- qkv_weight_grad: float32 [896, 1152], P('dp')
- qkv_bias_grad: float32 [1024], P('dp')
- value_bias_grad: float32 [128], P('dp')
- out_weight_grad: float32 [896, 896], P('dp')
- mlp_gain_grad: float32 [896], P('dp')
- gate_weight_grad: float32 [896, 4864], P('dp')
- up_weight_grad: float32 [896, 4864], P('dp')
- down_weight_grad: float32 [4864, 896], P('dp')
Inputs may be any that keep to these rules, and one draw needn't show every extreme that they name: `span_order`: entries 2c and 2c + 1 hold two spans j and 63 - j, in either order; every span appears once. `positions`: each token's position within its document. Documents are runs of consecutive places of a sequence, none longer than 1024 tokens, and positions count from 0 at a run's start, increasing by one along place.
All inputs are finite; a program needn't handle non-finite values.
Results may differ from a plain program's by a relative error of at most 0.03.
Values may be sent and summed in bfloat16 or wider, within the bound.
A program may use at most 192 MiB of HBM per device.

v0:
```python
import jax
import jax.numpy as jnp
from jax import lax
from jax.sharding import PartitionSpec as P

QH = 14
KVH = 2
HD = 64
norm_eps = 1e-06
rope_base = 1000000.0
masked_score = -1e30


def rms_apply(values, gain):
    mean_square = jnp.mean(values * values, axis=-1, keepdims=True)
    return values * lax.rsqrt(mean_square + norm_eps) * gain


def half_turn(values):
    middle = values.shape[-1] // 2
    return jnp.concatenate([-values[..., middle:], values[..., :middle]], axis=-1)


def rotate(values, cosine, sine):
    return values * cosine + half_turn(values) * sine


def rope_tables(positions, head_dim):
    middle = head_dim // 2
    inverse = rope_base ** (-(jnp.arange(middle).astype(jnp.float32) * 2.0) / head_dim)
    angles = positions.astype(jnp.float32)[:, None] * inverse[None, :]
    angles = jnp.concatenate([angles, angles], axis=-1)
    return (jnp.cos(angles), jnp.sin(angles))


def span_lookup(table, slots):
    picked = slots[:, None] == jnp.arange(table.shape[0], dtype=jnp.int32)[None, :]
    return jnp.sum(jnp.where(picked, table[None, :], 0), axis=1)


def swiglu(gate_in, up_in):
    return jax.nn.silu(gate_in) * up_in


def body(
    inputs,
    cotangent,
    span_order,
    positions,
    attn_gain,
    qkv_weight,
    qkv_bias,
    out_weight,
    mlp_gain,
    gate_weight,
    up_weight,
    down_weight,
):
    token_count = inputs.shape[0]
    span_rows = token_count // 2
    head_dim = HD
    query_heads = QH
    kv_heads = KVH
    group_size = query_heads // kv_heads
    score_scale = head_dim ** (-0.5)
    q_cols = query_heads * head_dim
    k_cols = kv_heads * head_dim
    seq_length = token_count * lax.axis_size("ctx")
    key_block = min(1024, seq_length)
    block_count = seq_length // key_block
    device_slot = lax.axis_index("ctx")
    local_slots = jnp.arange(token_count, dtype=jnp.int32)
    query_places = (
        span_lookup(span_order, 2 * device_slot + local_slots // span_rows) * span_rows
        + local_slots % span_rows
    )
    all_slots = jnp.arange(seq_length, dtype=jnp.int32)
    key_places = span_lookup(span_order, all_slots // span_rows) * span_rows + all_slots % span_rows
    key_places = key_places.reshape(block_count, key_block)
    gain_one, qkv_full, bias_full, out_full = (
        lax.all_gather(attn_gain, "dp", axis=0, tiled=True),
        lax.all_gather(qkv_weight, "dp", axis=0, tiled=True),
        lax.all_gather(qkv_bias, "dp", axis=0, tiled=True),
        lax.all_gather(out_weight, "dp", axis=0, tiled=True),
    )
    inputs_wide = inputs.astype(jnp.float32)
    gain_one_wide = gain_one.astype(jnp.float32)
    normed_one = rms_apply(inputs_wide, gain_one_wide).astype(jnp.bfloat16)
    mixed_proj = jnp.dot(
        normed_one, qkv_full, preferred_element_type=jnp.float32
    ) + bias_full.astype(jnp.float32)
    cosine, sine = rope_tables(positions, head_dim)
    cosine = cosine[:, None, :]
    sine = sine[:, None, :]
    query_rot = rotate(
        mixed_proj[:, :q_cols].reshape(token_count, query_heads, head_dim), cosine, sine
    ).astype(jnp.bfloat16)
    key_rot = rotate(
        mixed_proj[:, q_cols : q_cols + k_cols].reshape(token_count, kv_heads, head_dim),
        cosine,
        sine,
    )
    key_rot = key_rot.astype(jnp.bfloat16).reshape(token_count, k_cols)
    value_low = mixed_proj[:, q_cols + k_cols :].astype(jnp.bfloat16)
    key_all, value_all = (
        lax.all_gather(key_rot, "ctx", axis=0, tiled=True),
        lax.all_gather(value_low, "ctx", axis=0, tiled=True),
    )
    key_blocks = key_all.reshape(block_count, key_block, kv_heads, head_dim)
    value_blocks = value_all.reshape(block_count, key_block, kv_heads, head_dim)
    query_grouped = query_rot.reshape(token_count, kv_heads, group_size, head_dim)

    def block_scores(key_part, place_part):
        scores = (
            jnp.einsum(
                "qhgd,khd->hgqk", query_grouped, key_part, preferred_element_type=jnp.float32
            )
            * score_scale
        )
        allowed = place_part[None, :] <= query_places[:, None]
        return jnp.where(allowed[None, None], scores, masked_score)

    def max_step(running, pieces):
        running_max, running_sum = running
        scores = block_scores(pieces[0], pieces[1])
        new_max = jnp.maximum(running_max, jnp.max(scores, axis=-1))
        new_sum = running_sum * jnp.exp(running_max - new_max) + jnp.sum(
            jnp.exp(scores - new_max[..., None]), axis=-1
        )
        return ((new_max, new_sum), None)

    start_max = jnp.full((kv_heads, group_size, token_count), masked_score, jnp.float32)
    start_sum = jnp.zeros((kv_heads, group_size, token_count), jnp.float32)
    (final_max, final_sum), unused = lax.scan(
        max_step, (start_max, start_sum), (key_blocks, key_places)
    )
    log_total = final_max + jnp.log(final_sum)

    def value_step(attended_sum, pieces):
        scores = block_scores(pieces[0], pieces[2])
        probs_low = jnp.exp(scores - log_total[..., None]).astype(jnp.bfloat16)
        return (
            attended_sum
            + jnp.einsum(
                "hgqk,khd->qhgd", probs_low, pieces[1], preferred_element_type=jnp.float32
            ),
            None,
        )

    start_total = jnp.zeros((token_count, kv_heads, group_size, head_dim), jnp.float32)
    attended_sum, unused = lax.scan(value_step, start_total, (key_blocks, value_blocks, key_places))
    attended_low = attended_sum.reshape(token_count, q_cols).astype(jnp.bfloat16)
    residual = inputs_wide + jnp.dot(attended_low, out_full, preferred_element_type=jnp.float32)
    gain_two, gate_full, up_full, down_full = (
        lax.all_gather(mlp_gain, "dp", axis=0, tiled=True),
        lax.all_gather(gate_weight, "dp", axis=0, tiled=True),
        lax.all_gather(up_weight, "dp", axis=0, tiled=True),
        lax.all_gather(down_weight, "dp", axis=0, tiled=True),
    )
    gain_two_wide = gain_two.astype(jnp.float32)
    normed_two = rms_apply(residual, gain_two_wide).astype(jnp.bfloat16)
    gate_proj = jnp.dot(normed_two, gate_full, preferred_element_type=jnp.float32)
    up_proj = jnp.dot(normed_two, up_full, preferred_element_type=jnp.float32)
    hidden_low = swiglu(gate_proj, up_proj).astype(jnp.bfloat16)
    output = (residual + jnp.dot(hidden_low, down_full, preferred_element_type=jnp.float32)).astype(
        jnp.bfloat16
    )
    d_hidden = jnp.dot(cotangent, down_full.T, preferred_element_type=jnp.float32)
    down_grad = jnp.dot(hidden_low.T, cotangent, preferred_element_type=jnp.float32)
    swiglu_back = jax.vjp(swiglu, gate_proj, up_proj)[1]
    d_gate, d_up = swiglu_back(d_hidden)
    d_gate = d_gate.astype(jnp.bfloat16)
    d_up = d_up.astype(jnp.bfloat16)
    gate_grad = jnp.dot(normed_two.T, d_gate, preferred_element_type=jnp.float32)
    up_grad = jnp.dot(normed_two.T, d_up, preferred_element_type=jnp.float32)
    d_normed_two = jnp.dot(d_gate, gate_full.T, preferred_element_type=jnp.float32) + jnp.dot(
        d_up, up_full.T, preferred_element_type=jnp.float32
    )
    norm_two_back = jax.vjp(rms_apply, residual, gain_two_wide)[1]
    d_resid_part, gain_two_grad = norm_two_back(d_normed_two)
    d_residual = d_resid_part + cotangent.astype(jnp.float32)
    d_branch = d_residual.astype(jnp.bfloat16)
    out_grad = jnp.dot(attended_low.T, d_branch, preferred_element_type=jnp.float32)
    d_attended = jnp.dot(d_branch, out_full.T, preferred_element_type=jnp.float32).astype(
        jnp.bfloat16
    )
    d_attended = d_attended.reshape(token_count, kv_heads, group_size, head_dim)
    row_delta = jnp.einsum("qhgd,qhgd->hgq", d_attended.astype(jnp.float32), attended_sum)

    def grad_step(d_query, pieces):
        key_part, value_part, place_part = pieces
        scores = block_scores(key_part, place_part)
        probs_full = jnp.exp(scores - log_total[..., None])
        probs_low = probs_full.astype(jnp.bfloat16)
        d_probs = jnp.einsum(
            "qhgd,khd->hgqk", d_attended, value_part, preferred_element_type=jnp.float32
        )
        d_scores = (probs_full * (d_probs - row_delta[..., None])).astype(jnp.bfloat16)
        d_query = (
            d_query
            + jnp.einsum("hgqk,khd->qhgd", d_scores, key_part, preferred_element_type=jnp.float32)
            * score_scale
        )
        d_key = (
            jnp.einsum(
                "hgqk,qhgd->khd", d_scores, query_grouped, preferred_element_type=jnp.float32
            )
            * score_scale
        )
        d_value = jnp.einsum(
            "hgqk,qhgd->khd", probs_low, d_attended, preferred_element_type=jnp.float32
        )
        return (d_query, (d_key, d_value))

    d_query, (d_key_blocks, d_value_blocks) = lax.scan(
        grad_step, start_total, (key_blocks, value_blocks, key_places)
    )
    d_key_all = d_key_blocks.reshape(seq_length, k_cols)
    d_value_all = d_value_blocks.reshape(seq_length, k_cols)
    d_key_own, d_value_own = (
        lax.psum_scatter(
            d_key_all.astype(jnp.bfloat16), "ctx", scatter_dimension=0, tiled=True
        ).astype(jnp.float32),
        lax.psum_scatter(
            d_value_all.astype(jnp.bfloat16), "ctx", scatter_dimension=0, tiled=True
        ).astype(jnp.float32),
    )

    def turn_back(grads):
        return jax.vjp(lambda values: rotate(values, cosine, sine), grads)[1](grads)[0]

    d_query_raw = turn_back(d_query.reshape(token_count, query_heads, head_dim)).reshape(
        token_count, q_cols
    )
    d_key_raw = turn_back(d_key_own.reshape(token_count, kv_heads, head_dim)).reshape(
        token_count, k_cols
    )
    d_mixed = jnp.concatenate([d_query_raw, d_key_raw, d_value_own], axis=1).astype(jnp.bfloat16)
    qkv_grad = jnp.dot(normed_one.T, d_mixed, preferred_element_type=jnp.float32)
    bias_grad = jnp.sum(d_mixed.astype(jnp.float32), axis=0)
    qk_bias_grad = bias_grad[: q_cols + k_cols]
    value_bias_grad = bias_grad[q_cols + k_cols :]
    d_normed_one = jnp.dot(d_mixed, qkv_full.T, preferred_element_type=jnp.float32)
    norm_one_back = jax.vjp(rms_apply, inputs_wide, gain_one_wide)[1]
    d_input_part, gain_one_grad = norm_one_back(d_normed_one)
    input_grad = (d_input_part + d_residual).astype(jnp.bfloat16)
    local_grads = (
        gain_one_grad,
        qkv_grad,
        qk_bias_grad,
        value_bias_grad,
        out_grad,
        gain_two_grad,
        gate_grad,
        up_grad,
        down_grad,
    )
    shard_grads = (
        lax.psum_scatter(
            local_grads[0].astype(jnp.bfloat16), "dp", scatter_dimension=0, tiled=True
        ).astype(jnp.float32),
        lax.psum_scatter(
            local_grads[1].astype(jnp.bfloat16), "dp", scatter_dimension=0, tiled=True
        ).astype(jnp.float32),
        lax.psum_scatter(
            local_grads[2].astype(jnp.bfloat16), "dp", scatter_dimension=0, tiled=True
        ).astype(jnp.float32),
        lax.psum_scatter(
            local_grads[3].astype(jnp.bfloat16), "dp", scatter_dimension=0, tiled=True
        ).astype(jnp.float32),
        lax.psum_scatter(
            local_grads[4].astype(jnp.bfloat16), "dp", scatter_dimension=0, tiled=True
        ).astype(jnp.float32),
        lax.psum_scatter(
            local_grads[5].astype(jnp.bfloat16), "dp", scatter_dimension=0, tiled=True
        ).astype(jnp.float32),
        lax.psum_scatter(
            local_grads[6].astype(jnp.bfloat16), "dp", scatter_dimension=0, tiled=True
        ).astype(jnp.float32),
        lax.psum_scatter(
            local_grads[7].astype(jnp.bfloat16), "dp", scatter_dimension=0, tiled=True
        ).astype(jnp.float32),
        lax.psum_scatter(
            local_grads[8].astype(jnp.bfloat16), "dp", scatter_dimension=0, tiled=True
        ).astype(jnp.float32),
    )
    summed = (
        lax.psum(shard_grads[0].astype(jnp.bfloat16), "ctx").astype(jnp.float32),
        lax.psum(shard_grads[1].astype(jnp.bfloat16), "ctx").astype(jnp.float32),
        lax.psum(shard_grads[2].astype(jnp.bfloat16), "ctx").astype(jnp.float32),
        lax.psum(shard_grads[3].astype(jnp.bfloat16), "ctx").astype(jnp.float32),
        lax.psum(shard_grads[4].astype(jnp.bfloat16), "ctx").astype(jnp.float32),
        lax.psum(shard_grads[5].astype(jnp.bfloat16), "ctx").astype(jnp.float32),
        lax.psum(shard_grads[6].astype(jnp.bfloat16), "ctx").astype(jnp.float32),
        lax.psum(shard_grads[7].astype(jnp.bfloat16), "ctx").astype(jnp.float32),
        lax.psum(shard_grads[8].astype(jnp.bfloat16), "ctx").astype(jnp.float32),
    )
    return (
        output,
        input_grad,
        summed[0],
        summed[1],
        summed[2],
        summed[3],
        summed[4],
        summed[5],
        summed[6],
        summed[7],
        summed[8],
    )


def solution(mesh):
    placed = (
        P(("dp", "ctx"), None),
        P(("dp", "ctx"), None),
        P(),
        P(("dp", "ctx")),
        P("dp"),
        P("dp", None),
        P("dp"),
        P("dp", None),
        P("dp"),
        P("dp", None),
        P("dp", None),
        P("dp", None),
    )
    return jax.shard_map(
        body,
        mesh=mesh,
        in_specs=placed,
        out_specs=(
            P(("dp", "ctx"), None),
            P(("dp", "ctx"), None),
            P("dp"),
            P("dp", None),
            P("dp"),
            P("dp"),
            P("dp", None),
            P("dp"),
            P("dp", None),
            P("dp", None),
            P("dp", None),
        ),
        check_vma=False,
    )
```

profile of v0, /device:TPU:1, one launch (start us, length us, event | category | flops | bytes accessed | tf_op | source)
XLA Modules:
  0.0 1149.0 jit_solution(3470323007845369848)
XLA Ops:
  13.2 9.4 all-reduce.14
  23.7 19.9 %all-gather.8.cloned.1.call-done = bf16[896,1152]{1,0:T(8,128)(2,1)} async-done(((bf16[224,1152]{1,0:T(8,128)(2,1)}), bf16[896,1152]{1,0:T(8,128)(2,1)}) %all-gather.8.cloned.1.call-update) | async-done | bytes 2064400 | tf_op jit(solution)/shard_map/all_gather | solution.py:82
  51.1 38.8 %all-gather.10.cloned.1.call-done = bf16[4096,128]{1,0:T(8,128)(2,1)} async-done(((bf16[128,128]{1,0:T(8,128)(2,1)}), bf16[4096,128]{1,0:T(8,128)(2,1)}) %all-gather.10.cloned.1.call-update) | async-done | bytes 1048592 | tf_op jit(solution)/shard_map/all_gather | solution.py:107
  100.7 34.2 %all-gather.12.cloned.1.call-done = bf16[4096,128]{1,0:T(8,128)(2,1)} async-done(((bf16[128,128]{1,0:T(8,128)(2,1)}), bf16[4096,128]{1,0:T(8,128)(2,1)}) %all-gather.12.cloned.1.call-update) | async-done | bytes 1048592 | tf_op jit(solution)/shard_map/all_gather | solution.py:106
  144.5 37.0 %while.39 = (s32[]{:T(128)}, f32[2,7,128]{2,1,0:T(8,128)S(1)}, f32[2,7,128]{2,1,0:T(8,128)S(1)}, s32[4,1024]{1,0:T(4,128)S(1)}, s32[128]{0:T(128)S(1)}, /*index=...) while((s32[]{:T(128)}, f32[2,7,128]{2,1,0:T(8,128)S(1)}, ...), condition=%wide.region_6.7_spmd.clone, body=%wide.region_3.6_spmd.clone.sunk | while | flops 247866112 | bytes 15670904 | solution.py:134
  181.6 15.2 %while.40 = (s32[]{:T(128)}, f32[128,2,7,64]{0,3,2,1:T(8,128)S(1)}, bf16[4,1024,2,64]{1,3,2,0:T(8,128)(2,1)}, s32[4,1024]{1,0:T(4,128)S(1)}, s32[128]{0:T(128)S(...) while((s32[]{:T(128)}, f32[128,2,7,64]{0,3,2,1:T(8,128)S(1)}, ...), condition=%wide.region_8.9_spmd.clone, body=%wide.region_7.8_spmd.clone.sunk | while | flops 477462528 | bytes 1955962 | solution.py:151
  199.9 49.5 %all-gather.16.cloned.1.call-done = bf16[896,4864]{1,0:T(8,128)(2,1)} async-done(((bf16[224,4864]{1,0:T(8,128)(2,1)}), bf16[896,4864]{1,0:T(8,128)(2,1)}) %all-gather.16.cloned.1.call-update) | async-done | bytes 8716304 | tf_op jit(solution)/shard_map/all_gather | solution.py:156
  255.8 81.9 %all-gather.18.cloned.1.call-done = bf16[896,4864]{1,0:T(8,128)(2,1)} async-done(((bf16[224,4864]{1,0:T(8,128)(2,1)}), bf16[896,4864]{1,0:T(8,128)(2,1)}) %all-gather.18.cloned.1.call-update) | async-done | bytes 8716304 | tf_op jit(solution)/shard_map/all_gather | solution.py:157
  337.7 6.4 fusion.103
  344.1 82.1 %all-gather.20.cloned.1.call-done = bf16[4864,896]{1,0:T(8,128)(2,1)} async-done(((bf16[1216,896]{1,0:T(8,128)(2,1)}), bf16[4864,896]{1,0:T(8,128)(2,1)}) %all-gather.20.cloned.1.call-update) | async-done | bytes 8716304 | tf_op jit(solution)/shard_map/all_gather | solution.py:158
  426.3 7.5 multiply_convert_fusion
  433.8 7.2 fusion.104
  449.2 71.3 %while.41 = (s32[]{:T(128)}, f32[128,2,7,64]{0,3,2,1:T(8,128)S(1)}, bf16[4,1024,2,64]{1,3,2,0:T(8,128)(2,1)}, bf16[4,1024,2,64]{1,3,2,0:T(8,128)(2,1)}, bf16[4,1...) while((s32[]{:T(128)}, f32[128,2,7,64]{0,3,2,1:T(8,128)S(1)}, ...), condition=%wide.region_12.13_spmd.clone, body=%wide.region_11.12_spmd.clone.sunk | while | flops 1193361408 | bytes 99781520 | solution.py:215
  544.2 64.3 %reduce-scatter.24.cloned.1.call-done = bf16[128,128]{1,0:T(8,128)(2,1)} async-done(((bf16[4096,128]{1,0:T(8,128)(2,1)}), bf16[128,128]{1,0:T(8,128)(2,1)}) %reduce-scatter.24.cloned.1.call-update) | async-done | bytes 32784
  609.3 80.0 %reduce-scatter.22.cloned.1.call-done = bf16[128,128]{1,0:T(8,128)(2,1)} async-done(((bf16[4096,128]{1,0:T(8,128)(2,1)}), bf16[128,128]{1,0:T(8,128)(2,1)}) %reduce-scatter.22.cloned.1.call-update) | async-done | bytes 32784
  692.7 7.2 convolution_convert_fusion.2
  699.9 7.2 convolution_convert_fusion.1
  718.2 32.8 %reduce-scatter.12.cloned.1.call-done = bf16[224,1152]{1,0:T(8,128)(2,1)} async-done(((bf16[896,1152]{1,0:T(8,128)(2,1)}), bf16[224,1152]{1,0:T(8,128)(2,1)}) %reduce-scatter.12.cloned.1.call-update) | async-done | bytes 516112 | tf_op jit(solution)/shard_map/reduce_scatter | solution.py:262
  751.0 85.4 %reduce-scatter.16.cloned.1.call-done = bf16[224,4864]{1,0:T(8,128)(2,1)} async-done(((bf16[896,4864]{1,0:T(8,128)(2,1)}), bf16[224,4864]{1,0:T(8,128)(2,1)}) %reduce-scatter.16.cloned.1.call-update) | async-done | bytes 2179088 | tf_op jit(solution)/shard_map/reduce_scatter | solution.py:277
  836.4 85.4 %reduce-scatter.18.cloned.1.call-done = bf16[224,4864]{1,0:T(8,128)(2,1)} async-done(((bf16[896,4864]{1,0:T(8,128)(2,1)}), bf16[224,4864]{1,0:T(8,128)(2,1)}) %reduce-scatter.18.cloned.1.call-update) | async-done | bytes 2179088 | tf_op jit(solution)/shard_map/reduce_scatter | solution.py:280
  921.7 85.4 %reduce-scatter.20.cloned.1.call-done = bf16[1216,896]{1,0:T(8,128)(2,1)} async-done(((bf16[4864,896]{1,0:T(8,128)(2,1)}), bf16[1216,896]{1,0:T(8,128)(2,1)}) %reduce-scatter.20.cloned.1.call-update) | async-done | bytes 2179088 | tf_op jit(solution)/shard_map/reduce_scatter | solution.py:283
  1016.0 7.1 all-reduce.13
  1023.4 65.2 %all-reduce.11 = (bf16[224]{0:T(256)(128)(2,1)S(1)}, bf16[256]{0:T(256)(128)(2,1)S(1)}, bf16[32]{0:T(256)(128)(2,1)S(1)}, bf16[224]{0:T(256)(128)(2,1)S(1)}) all-reduce(bf16[224]{0:T(256)(128)(2,1)S(1)} %dynamic-slice.4, bf16[256]{0:T(256)(128)(2,1)S(1)} %dynamic-slice.6, ...), channel_id=1, replica_groups=mesh['dp'=4,'ctx'=32] {'ctx'}, use_global_device_ids=true, to_apply=%region_18.19 | all-reduce | flops 736 | bytes 2944 | tf_op jit(solution)/shard_map/psum | solution.py:288
  1091.7 39.1 %all-reduce.17.cloned.1.call-done = (bf16[224,1152]{1,0:T(8,128)(2,1)}, bf16[224,896]{1,0:T(8,128)(2,1)}, bf16[224,4864]{1,0:T(8,128)(2,1)}, bf16[224,4864]{1,0:T(8,128)(2,1)}, bf16[1216,896]{1,0:T(8,128)(2,1)}) async-done(((bf16[224,1152]{1,0:T(8,128)(2,1)}, bf16[224,896]{1,0:T(8,128)(2,1)}, bf16[224,4864]{1,0:T(8,128)(2,1)}, bf16[224,4864]{1,0:T(8,128)(2,1)}, bf16[1216,896]{1,0:T(8,128)(2,1)}), ...) | async-done | bytes 7454736 | tf_op jit(solution)/shard_map/psum | solution.py:289
  (307 shorter events, 233.6 us)
Async XLA Ops:
  7.2 39.3 %copy-start.31 = (s32[128]{0:T(128)S(1)}, s32[128]{0:T(128)}, u32[]{:S(2)}) copy-start(s32[128]{0:T(128)} %param.21) | copy-start | bytes 1540
  7.2 36.4 %all-gather.8.cloned.1.call-start = ((), (), s32[]{:S(2)}) async-start(), calls=%async_computation.7 | async-start | bytes 2580480 | tf_op jit(solution)/shard_map/all_gather | solution.py:82
  7.9 82.0 %all-gather.10.cloned.1.call-start = ((), (), s32[]{:S(2)}) async-start(), calls=%async_computation.8 | async-start | bytes 1081344 | tf_op jit(solution)/shard_map/all_gather | solution.py:107
  23.7 23.3 %copy-start.29 = (f32[128]{0:T(128)}, f32[128]{0:T(128)S(1)}, u32[]{:S(2)}) copy-start(f32[128]{0:T(128)S(1)} %fusion.73) | copy-start | bytes 1540
  46.5 88.4 %all-gather.12.cloned.1.call-start = ((), (), s32[]{:S(2)}) async-start(), calls=%async_computation.9 | async-start | bytes 1081344 | tf_op jit(solution)/shard_map/all_gather | solution.py:106
  47.7 149.1 %all-gather.14.cloned.1.call-start = ((), (), s32[]{:S(2)}) async-start(), calls=%async_computation.10 | async-start | bytes 2007040 | tf_op jit(solution)/shard_map/all_gather | solution.py:84
  48.3 201.1 %all-gather.16.cloned.1.call-start = ((), (), s32[]{:S(2)}) async-start(), calls=%async_computation.11 | async-start | bytes 10895360 | tf_op jit(solution)/shard_map/all_gather | solution.py:156
  48.9 288.8 %all-gather.18.cloned.1.call-start = ((), (), s32[]{:S(2)}) async-start(), calls=%async_computation.12 | async-start | bytes 10895360 | tf_op jit(solution)/shard_map/all_gather | solution.py:157
  49.5 376.8 %all-gather.20.cloned.1.call-start = ((), (), s32[]{:S(2)}) async-start(), calls=%async_computation.13 | async-start | bytes 10895360 | tf_op jit(solution)/shard_map/all_gather | solution.py:158
  50.2 558.2 %reduce-scatter.24.cloned.1.call-start = ((), (), s32[]{:S(2)}) async-start(), calls=%async_computation.20 | async-start | bytes 1081344
  181.5 15.3 %copy-start.9 = (bf16[128,896]{1,0:T(8,128)(2,1)S(1)}, bf16[128,896]{1,0:T(8,128)(2,1)}, u32[]{:S(2)}) copy-start(bf16[128,896]{1,0:T(8,128)(2,1)} %param.18) | copy-start | bytes 688132
  196.7 59.0 %copy-start.19 = (f32[128,2,7,64]{0,3,2,1:T(8,128)}, f32[128,2,7,64]{0,3,2,1:T(8,128)S(1)}, u32[]{:S(2)}) copy-start(f32[128,2,7,64]{0,3,2,1:T(8,128)S(1)} %get-tuple-element.157) | copy-start | bytes 1376260
  196.8 59.0 %copy-start.17 = (bf16[128,2,7,64]{0,3,2,1:T(8,128)(2,1)}, bf16[128,2,7,64]{0,3,2,1:T(8,128)(2,1)S(1)}, u32[]{:S(2)}) copy-start(bf16[128,2,7,64]{0,3,2,1:T(8,128)(2,1)S(1)} %convert_element_type.171) | copy-start | bytes 688132
  531.2 158.1 %reduce-scatter.22.cloned.1.call-start = ((), (), s32[]{:S(2)}) async-start(), calls=%async_computation.19 | async-start | bytes 1081344
  531.3 10.9 copy-start.7
  531.3 10.9 copy-start.18
  542.1 148.1 %copy-start.10 = (bf16[128,896]{1,0:T(8,128)(2,1)S(1)}, bf16[128,896]{1,0:T(8,128)(2,1)}, u32[]{:S(2)}) copy-start(bf16[128,896]{1,0:T(8,128)(2,1)} %param.18) | copy-start | bytes 688132
  542.1 176.0 %reduce-scatter.14.cloned.1.call-start = ((), (), s32[]{:S(2)}) async-start(), calls=%async_computation.15 | async-start | bytes 2007040 | tf_op jit(solution)/shard_map/reduce_scatter | solution.py:271
  543.9 207.0 %reduce-scatter.12.cloned.1.call-start = ((), (), s32[]{:S(2)}) async-start(), calls=%async_computation.14 | async-start | bytes 2580480 | tf_op jit(solution)/shard_map/reduce_scatter | solution.py:262
  692.4 144.0 %reduce-scatter.16.cloned.1.call-start = ((), (), s32[]{:S(2)}) async-start(), calls=%async_computation.16 | async-start | bytes 10895360 | tf_op jit(solution)/shard_map/reduce_scatter | solution.py:277
  699.8 221.9 %reduce-scatter.18.cloned.1.call-start = ((), (), s32[]{:S(2)}) async-start(), calls=%async_computation.17 | async-start | bytes 10895360 | tf_op jit(solution)/shard_map/reduce_scatter | solution.py:280
  707.1 300.0 %reduce-scatter.20.cloned.1.call-start = ((), (), s32[]{:S(2)}) async-start(), calls=%async_computation.18 | async-start | bytes 10895360 | tf_op jit(solution)/shard_map/reduce_scatter | solution.py:283
  712.8 418.0 %all-reduce.17.cloned.1.call-start = ((), (), s32[]{:S(2)}) async-start(), calls=%async_computation.21 | async-start | bytes 14909440 | tf_op jit(solution)/shard_map/psum | solution.py:289
  1014.9 75.9 %copy-start.30 = (f32[128]{0:T(128)S(1)}, f32[128]{0:T(128)}, u32[]{:S(2)}) copy-start(f32[128]{0:T(128)} %copy-done.29) | copy-start | bytes 1540
  (47 other events, 178.0 us)
Sparse Core Ops, SparseCore 0:
  9.7 33.8 all-gather.7
  46.6 43.2 all-gather.9
  92.8 42.0 all-gather.11
  136.4 25.5 all-gather.13
  163.5 85.8 all-gather.15
  250.9 86.7 all-gather.17
  339.4 86.8 all-gather.19
  531.4 77.0 reduce-scatter.23
  612.4 76.9 reduce-scatter.21
  692.2 25.9 reduce-scatter.13
  721.2 29.7 reduce-scatter.11
  753.5 82.8 reduce-scatter.15
  838.8 82.8 reduce-scatter.17
  924.2 82.8 reduce-scatter.19
  1011.1 119.6 all-reduce.16
where the time goes:
time: 1160 us; the launch traced here: 1150 us
  waiting for transfers between devices  787 us (68%)
  matrix products  160 us (14%)
  blocking collectives  81.7 us (7%)
  local copies, waits for them, and re-layouts  59.3 us (5%)
  other arithmetic  40.1 us (3%)
  between operations  18.1 us (2%)
    unnamed x17, waiting for transfers between devices  147 us
    reduce_scatter x1, waiting for transfers between devices, body(): lax.psum_scatter(local_grads[6].astype(jnp.bfloat16), 'dp', scatter_dimen...  85.4 us
    reduce_scatter x1, waiting for transfers between devices, body(): lax.psum_scatter(local_grads[8].astype(jnp.bfloat16), 'dp', scatter_dimen...  85.4 us
    reduce_scatter x1, waiting for transfers between devices, body(): lax.psum_scatter(local_grads[7].astype(jnp.bfloat16), 'dp', scatter_dimen...  85.4 us
    all_gather x1, waiting for transfers between devices, body(): lax.all_gather(down_weight, 'dp', axis=0, tiled=True)  82.1 us
    all_gather x1, waiting for transfers between devices, body(): lax.all_gather(up_weight, 'dp', axis=0, tiled=True)  81.9 us
    psum x1, blocking collectives, body(): lax.psum(shard_grads[0].astype(jnp.bfloat16), 'ctx').astype(jnp.float32)  65.2 us
    all_gather x1, waiting for transfers between devices, body(): lax.all_gather(gate_weight, 'dp', axis=0, tiled=True)  49.5 us
  transfers between devices with their start and end apart: 15, of which 14 were waited for; matrix products, arithmetic and copies ran while one was open for 12% of the time, Pallas kernels for 0%

commit v1 on v0

--- a/solution.py
+++ b/solution.py
@@ -9,6 +9,11 @@
 norm_eps = 1e-06
 rope_base = 1000000.0
 masked_score = -1e30
+
+
+def swapped_in(x, name, d):
+    stack = jnp.stack([x] * lax.axis_size(name))
+    return jnp.concatenate(lax.all_to_all(stack, name, 0, 0), axis=d)
 
 
 def rms_apply(values, gain):
@@ -103,7 +108,7 @@
     key_rot = key_rot.astype(jnp.bfloat16).reshape(token_count, k_cols)
     value_low = mixed_proj[:, q_cols + k_cols :].astype(jnp.bfloat16)
     key_all, value_all = (
-        lax.all_gather(key_rot, "ctx", axis=0, tiled=True),
+        swapped_in(key_rot, "ctx", 0),
         lax.all_gather(value_low, "ctx", axis=0, tiled=True),
     )
     key_blocks = key_all.reshape(block_count, key_block, kv_heads, head_dim)

time: 1160 us -> 1120 us (0.966)
  waiting for transfers between devices: 787 us -> 746 us
    all_gather x1, waiting for transfers between devices: 38.8 us -> 0.02 us  [body(): lax.all_gather(value_low, 'ctx', axis=0, tiled=True)]
    all_gather x1 -> x0, waiting for transfers between devices: 34.2 us -> none  [body(): lax.all_gather(key_rot, 'ctx', axis=0, tiled=True)]
    all_to_all x0 -> x1, waiting for transfers between devices: none -> 17 us  [swapped_in(): return jnp.concatenate(lax.all_to_all(stack, name, 0, 0), axis=d)]
    all_gather x1, waiting for transfers between devices: 49.5 us -> 64.4 us  [body(): lax.all_gather(gate_weight, 'dp', axis=0, tiled=True)]
    unnamed x17 -> x16, waiting for transfers between devices: 147 us -> 147 us
  transfers between devices with their start and end apart: 15 -> 15, of which waited for: 14 -> 13; matrix products, arithmetic and copies ran while one was open for 12% -> 12% of each run, Pallas kernels for 0% -> 0%
where the time goes in v1:
time: 1120 us; the launch traced here: 1110 us
  waiting for transfers between devices  746 us (67%)
  matrix products  160 us (14%)
  blocking collectives  81.6 us (7%)
  local copies, waits for them, and re-layouts  54.4 us (5%)
  other arithmetic  39.2 us (4%)
  between operations  18.2 us (2%)
    unnamed x16, waiting for transfers between devices  147 us
    reduce_scatter x1, waiting for transfers between devices, body(): lax.psum_scatter(local_grads[6].astype(jnp.bfloat16), 'dp', scatter_dimen...  85.5 us
    reduce_scatter x1, waiting for transfers between devices, body(): lax.psum_scatter(local_grads[8].astype(jnp.bfloat16), 'dp', scatter_dimen...  85.5 us
    reduce_scatter x1, waiting for transfers between devices, body(): lax.psum_scatter(local_grads[7].astype(jnp.bfloat16), 'dp', scatter_dimen...  85.2 us
    all_gather x1, waiting for transfers between devices, body(): lax.all_gather(down_weight, 'dp', axis=0, tiled=True)  82 us
    all_gather x1, waiting for transfers between devices, body(): lax.all_gather(up_weight, 'dp', axis=0, tiled=True)  82 us
    psum x1, blocking collectives, body(): lax.psum(shard_grads[0].astype(jnp.bfloat16), 'ctx').astype(jnp.float32)  65.2 us
    all_gather x1, waiting for transfers between devices, body(): lax.all_gather(gate_weight, 'dp', axis=0, tiled=True)  64.4 us
  transfers between devices with their start and end apart: 15, of which 13 were waited for; matrix products, arithmetic and copies ran while one was open for 12% of the time, Pallas kernels for 0%

profile of v1, /device:TPU:1, one launch (start us, length us, event | category | flops | bytes accessed | tf_op | source)
XLA Modules:
  0.0 1109.0 jit_solution(2735556663232730251)
XLA Ops:
  13.2 9.4 all-reduce.14
  23.7 19.9 %all-gather.7.cloned.1.call-done = bf16[896,1152]{1,0:T(8,128)(2,1)} async-done(((bf16[224,1152]{1,0:T(8,128)(2,1)}), bf16[896,1152]{1,0:T(8,128)(2,1)}) %all-gather.7.cloned.1.call-update) | async-done | bytes 2064400 | tf_op jit(solution)/shard_map/all_gather | solution.py:87
  51.2 7.6 all-to-all-start
  59.4 17.0 %all-to-all-done = bf16[32,128,128]{1,2,0:T(8,128)(2,1)S(1)} async-done(((bf16[32,128,128]{1,2,0:T(8,128)(2,1)}), bf16[32,128,128]{1,2,0:T(8,128)(2,1)S(1)}, u32[]{:S(2)}, u32[]{:S(2)}) %all-to-all-start) | async-done | bytes 1048608 | tf_op jit(solution)/shard_map/all_to_all | solution.py:16
  79.7 36.1 %while.39 = (s32[]{:T(128)}, f32[2,7,128]{2,1,0:T(8,128)S(1)}, f32[2,7,128]{2,1,0:T(8,128)S(1)}, s32[4,1024]{1,0:T(4,128)S(1)}, s32[128]{0:T(128)S(1)}, /*index=...) while((s32[]{:T(128)}, f32[2,7,128]{2,1,0:T(8,128)S(1)}, ...), condition=%wide.region_6.7_spmd.clone, body=%wide.region_3.6_spmd.clone.sunk | while | flops 247866112 | bytes 15670904 | solution.py:139
  126.8 15.2 %while.40 = (s32[]{:T(128)}, f32[128,2,7,64]{0,3,2,1:T(8,128)S(1)}, bf16[4,1024,2,64]{1,3,2,0:T(8,128)(2,1)}, s32[4,1024]{1,0:T(4,128)S(1)}, s32[128]{0:T(128)S(...) while((s32[]{:T(128)}, f32[128,2,7,64]{0,3,2,1:T(8,128)S(1)}, ...), condition=%wide.region_8.9_spmd.clone, body=%wide.region_7.8_spmd.clone.sunk | while | flops 477462528 | bytes 1955962 | solution.py:156
  145.1 64.4 %all-gather.13.cloned.1.call-done = bf16[896,4864]{1,0:T(8,128)(2,1)} async-done(((bf16[224,4864]{1,0:T(8,128)(2,1)}), bf16[896,4864]{1,0:T(8,128)(2,1)}) %all-gather.13.cloned.1.call-update) | async-done | bytes 8716304 | tf_op jit(solution)/shard_map/all_gather | solution.py:161
  209.5 6.4 fusion.102
  215.9 82.0 %all-gather.15.cloned.1.call-done = bf16[896,4864]{1,0:T(8,128)(2,1)} async-done(((bf16[224,4864]{1,0:T(8,128)(2,1)}), bf16[896,4864]{1,0:T(8,128)(2,1)}) %all-gather.15.cloned.1.call-update) | async-done | bytes 8716304 | tf_op jit(solution)/shard_map/all_gather | solution.py:162
  304.3 82.0 %all-gather.17.cloned.1.call-done = bf16[4864,896]{1,0:T(8,128)(2,1)} async-done(((bf16[1216,896]{1,0:T(8,128)(2,1)}), bf16[4864,896]{1,0:T(8,128)(2,1)}) %all-gather.17.cloned.1.call-update) | async-done | bytes 8716304 | tf_op jit(solution)/shard_map/all_gather | solution.py:163
  386.3 7.5 multiply_convert_fusion
  393.8 7.2 fusion.104
  409.2 71.4 %while.41 = (s32[]{:T(128)}, f32[128,2,7,64]{0,3,2,1:T(8,128)S(1)}, bf16[4,1024,2,64]{1,3,2,0:T(8,128)(2,1)}, bf16[4,1024,2,64]{1,3,2,0:T(8,128)(2,1)}, bf16[4,1...) while((s32[]{:T(128)}, f32[128,2,7,64]{0,3,2,1:T(8,128)S(1)}, ...), condition=%wide.region_12.13_spmd.clone, body=%wide.region_11.12_spmd.clone.sunk | while | flops 1193361408 | bytes 99781520 | solution.py:220
  504.2 64.3 %reduce-scatter.24.cloned.1.call-done = bf16[128,128]{1,0:T(8,128)(2,1)} async-done(((bf16[4096,128]{1,0:T(8,128)(2,1)}), bf16[128,128]{1,0:T(8,128)(2,1)}) %reduce-scatter.24.cloned.1.call-update) | async-done | bytes 32784
  569.4 80.0 %reduce-scatter.22.cloned.1.call-done = bf16[128,128]{1,0:T(8,128)(2,1)} async-done(((bf16[4096,128]{1,0:T(8,128)(2,1)}), bf16[128,128]{1,0:T(8,128)(2,1)}) %reduce-scatter.22.cloned.1.call-update) | async-done | bytes 32784
  652.7 7.2 convolution_convert_fusion.2
  659.9 7.2 convolution_convert_fusion.1
  678.5 32.6 %reduce-scatter.12.cloned.1.call-done = bf16[224,1152]{1,0:T(8,128)(2,1)} async-done(((bf16[896,1152]{1,0:T(8,128)(2,1)}), bf16[224,1152]{1,0:T(8,128)(2,1)}) %reduce-scatter.12.cloned.1.call-update) | async-done | bytes 516112 | tf_op jit(solution)/shard_map/reduce_scatter | solution.py:267
  711.0 85.5 %reduce-scatter.16.cloned.1.call-done = bf16[224,4864]{1,0:T(8,128)(2,1)} async-done(((bf16[896,4864]{1,0:T(8,128)(2,1)}), bf16[224,4864]{1,0:T(8,128)(2,1)}) %reduce-scatter.16.cloned.1.call-update) | async-done | bytes 2179088 | tf_op jit(solution)/shard_map/reduce_scatter | solution.py:282
  796.5 85.2 %reduce-scatter.18.cloned.1.call-done = bf16[224,4864]{1,0:T(8,128)(2,1)} async-done(((bf16[896,4864]{1,0:T(8,128)(2,1)}), bf16[224,4864]{1,0:T(8,128)(2,1)}) %reduce-scatter.18.cloned.1.call-update) | async-done | bytes 2179088 | tf_op jit(solution)/shard_map/reduce_scatter | solution.py:285
  881.8 85.5 %reduce-scatter.20.cloned.1.call-done = bf16[1216,896]{1,0:T(8,128)(2,1)} async-done(((bf16[4864,896]{1,0:T(8,128)(2,1)}), bf16[1216,896]{1,0:T(8,128)(2,1)}) %reduce-scatter.20.cloned.1.call-update) | async-done | bytes 2179088 | tf_op jit(solution)/shard_map/reduce_scatter | solution.py:288
  976.2 7.0 all-reduce.13
  983.6 65.2 %all-reduce.11 = (bf16[224]{0:T(256)(128)(2,1)S(1)}, bf16[256]{0:T(256)(128)(2,1)S(1)}, bf16[32]{0:T(256)(128)(2,1)S(1)}, bf16[224]{0:T(256)(128)(2,1)S(1)}) all-reduce(bf16[224]{0:T(256)(128)(2,1)S(1)} %dynamic-slice.4, bf16[256]{0:T(256)(128)(2,1)S(1)} %dynamic-slice.6, ...), channel_id=1, replica_groups=mesh['dp'=4,'ctx'=32] {'ctx'}, use_global_device_ids=true, to_apply=%region_18.19 | all-reduce | flops 736 | bytes 2944 | tf_op jit(solution)/shard_map/psum | solution.py:293
  1051.8 38.9 %all-reduce.17.cloned.1.call-done = (bf16[224,1152]{1,0:T(8,128)(2,1)}, bf16[224,896]{1,0:T(8,128)(2,1)}, bf16[224,4864]{1,0:T(8,128)(2,1)}, bf16[224,4864]{1,0:T(8,128)(2,1)}, bf16[1216,896]{1,0:T(8,128)(2,1)}) async-done(((bf16[224,1152]{1,0:T(8,128)(2,1)}, bf16[224,896]{1,0:T(8,128)(2,1)}, bf16[224,4864]{1,0:T(8,128)(2,1)}, bf16[224,4864]{1,0:T(8,128)(2,1)}, bf16[1216,896]{1,0:T(8,128)(2,1)}), ...) | async-done | bytes 7454736 | tf_op jit(solution)/shard_map/psum | solution.py:294
  (309 shorter events, 227.4 us)
Async XLA Ops:
  7.2 36.4 %all-gather.7.cloned.1.call-start = ((), (), s32[]{:S(2)}) async-start(), calls=%async_computation.8 | async-start | bytes 2580480 | tf_op jit(solution)/shard_map/all_gather | solution.py:87
  7.9 108.0 %all-gather.9.cloned.1.call-start = ((), (), s32[]{:S(2)}) async-start(), calls=%async_computation.9 | async-start | bytes 1081344 | tf_op jit(solution)/shard_map/all_gather | solution.py:112
  23.6 24.7 %copy-start.29 = (f32[128]{0:T(128)}, f32[128]{0:T(128)S(1)}, u32[]{:S(2)}) copy-start(f32[128]{0:T(128)S(1)} %fusion.73) | copy-start | bytes 1540
  46.5 95.6 %all-gather.11.cloned.1.call-start = ((), (), s32[]{:S(2)}) async-start(), calls=%async_computation.10 | async-start | bytes 2007040 | tf_op jit(solution)/shard_map/all_gather | solution.py:89
  47.2 162.3 %all-gather.13.cloned.1.call-start = ((), (), s32[]{:S(2)}) async-start(), calls=%async_computation.11 | async-start | bytes 10895360 | tf_op jit(solution)/shard_map/all_gather | solution.py:161
  47.8 250.1 %all-gather.15.cloned.1.call-start = ((), (), s32[]{:S(2)}) async-start(), calls=%async_computation.12 | async-start | bytes 10895360 | tf_op jit(solution)/shard_map/all_gather | solution.py:162
  48.4 337.9 %all-gather.17.cloned.1.call-start = ((), (), s32[]{:S(2)}) async-start(), calls=%async_computation.13 | async-start | bytes 10895360 | tf_op jit(solution)/shard_map/all_gather | solution.py:163
  51.2 25.2 %all-to-all-start = ((bf16[32,128,128]{1,2,0:T(8,128)(2,1)}), bf16[32,128,128]{1,2,0:T(8,128)(2,1)S(1)}, u32[]{:S(2)}, u32[]{:S(2)}) async-start(bf16[32,128,128]{1,2,0:T(8,128)(2,1)} %stack.3), calls=%async_computation | async-start | bytes 2097152 | tf_op jit(solution)/shard_map/all_to_all | solution.py:16
  58.9 509.6 %reduce-scatter.24.cloned.1.call-start = ((), (), s32[]{:S(2)}) async-start(), calls=%async_computation.20 | async-start | bytes 1081344
  126.8 15.3 %copy-start.9 = (bf16[128,896]{1,0:T(8,128)(2,1)S(1)}, bf16[128,896]{1,0:T(8,128)(2,1)}, u32[]{:S(2)}) copy-start(bf16[128,896]{1,0:T(8,128)(2,1)} %param.18) | copy-start | bytes 688132
  142.0 73.9 %copy-start.17 = (bf16[128,2,7,64]{0,3,2,1:T(8,128)(2,1)}, bf16[128,2,7,64]{0,3,2,1:T(8,128)(2,1)S(1)}, u32[]{:S(2)}) copy-start(bf16[128,2,7,64]{0,3,2,1:T(8,128)(2,1)S(1)} %convert_element_type.172) | copy-start | bytes 688132
  393.8 7.2 copy-start.12
  393.8 7.2 copy-start.11
  491.3 158.1 %reduce-scatter.22.cloned.1.call-start = ((), (), s32[]{:S(2)}) async-start(), calls=%async_computation.19 | async-start | bytes 1081344
  491.3 10.9 copy-start.7
  491.4 10.9 copy-start.18
  502.1 148.1 %copy-start.10 = (bf16[128,896]{1,0:T(8,128)(2,1)S(1)}, bf16[128,896]{1,0:T(8,128)(2,1)}, u32[]{:S(2)}) copy-start(bf16[128,896]{1,0:T(8,128)(2,1)} %param.18) | copy-start | bytes 688132
  502.2 176.3 %reduce-scatter.14.cloned.1.call-start = ((), (), s32[]{:S(2)}) async-start(), calls=%async_computation.15 | async-start | bytes 2007040 | tf_op jit(solution)/shard_map/reduce_scatter | solution.py:276
  504.0 207.0 %reduce-scatter.12.cloned.1.call-start = ((), (), s32[]{:S(2)}) async-start(), calls=%async_computation.14 | async-start | bytes 2580480 | tf_op jit(solution)/shard_map/reduce_scatter | solution.py:267
  652.4 144.1 %reduce-scatter.16.cloned.1.call-start = ((), (), s32[]{:S(2)}) async-start(), calls=%async_computation.16 | async-start | bytes 10895360 | tf_op jit(solution)/shard_map/reduce_scatter | solution.py:282
  659.9 221.9 %reduce-scatter.18.cloned.1.call-start = ((), (), s32[]{:S(2)}) async-start(), calls=%async_computation.17 | async-start | bytes 10895360 | tf_op jit(solution)/shard_map/reduce_scatter | solution.py:285
  667.2 300.1 %reduce-scatter.20.cloned.1.call-start = ((), (), s32[]{:S(2)}) async-start(), calls=%async_computation.18 | async-start | bytes 10895360 | tf_op jit(solution)/shard_map/reduce_scatter | solution.py:288
  672.9 417.9 %all-reduce.17.cloned.1.call-start = ((), (), s32[]{:S(2)}) async-start(), calls=%async_computation.21 | async-start | bytes 14909440 | tf_op jit(solution)/shard_map/psum | solution.py:294
  975.1 75.8 %copy-start.30 = (f32[128]{0:T(128)S(1)}, f32[128]{0:T(128)}, u32[]{:S(2)}) copy-start(f32[128]{0:T(128)} %copy-done.29) | copy-start | bytes 1540
  (47 other events, 169.2 us)
Sparse Core Ops, SparseCore 0:
  9.7 33.8 all-gather.6
  46.6 48.2 all-gather.8
  96.6 25.5 all-gather.10
  123.7 85.8 all-gather.12
  211.0 86.8 all-gather.14
  299.4 86.8 all-gather.16
  491.4 77.0 reduce-scatter.23
  572.4 76.9 reduce-scatter.21
  652.4 26.0 reduce-scatter.13
  681.3 29.6 reduce-scatter.11
  713.7 82.8 reduce-scatter.15
  798.9 82.8 reduce-scatter.17
  884.4 82.8 reduce-scatter.19
  971.3 119.3 all-reduce.16
